TPU v7x, 256 devices: a whole 4x4x8 slice. The times are simulated.
256 devices in a mesh: dom: 32 (over x_hi, z, core), sub: 8 (over x_lo, y).
Axes of the slice: x: 4 (x_hi: 2, x_lo: 2; x = x_hi * 2 + x_lo), y: 4, z: 8, core: 2. Of those that a mesh axis runs over, the one named last changes fastest.
Arguments:
- particles: float32 [3072, 4096], P('dom', 'sub'), may hold values from -6 to 6
- gradient: float32 [3072, 4096], P('dom', 'sub'), may hold values from -0.012 to 0.012
- curvature: float32 [4096], P('sub'), may hold values from 0.0005 to 0.004
Outputs:
- moved: float32 [3072, 4096], P('dom', 'sub')
All inputs are finite; a program needn't handle non-finite values.
Results may differ from a plain program's by a relative error of at most 0.000051.
Values sent between devices are 32-bit elements; how exact they have to be, the bound alone decides.
A program may use at most 64 MiB of HBM per device.

v0:
```python
import jax
import jax.numpy as jnp
from jax import lax
from jax.sharding import PartitionSpec as P


def pair_part(local, piece):
    local_norms = jnp.sum(local * local, axis=1)
    piece_norms = jnp.sum(piece * piece, axis=1)
    inner = jnp.dot(
        local, piece.T, precision=lax.Precision.HIGHEST, preferred_element_type=jnp.float32
    )
    return local_norms[:, None] + piece_norms[None, :] - 2.0 * inner


def stein_step(coords, grads):
    count = coords.shape[0] * lax.axis_size("dom")
    first, second = lax.psum((jnp.sum(coords, axis=0), jnp.sum(coords * coords)), "dom")
    first_sq = jnp.sum(first * first)
    whole_coords, whole_grads = (
        lax.all_gather(coords, "dom", axis=0, tiled=True),
        lax.all_gather(grads, "dom", axis=0, tiled=True),
    )
    partial_dist = pair_part(coords, whole_coords)
    second_all, first_all = lax.psum((second, first_sq), "sub")
    dist = lax.psum(partial_dist, "sub")
    width = (
        (2.0 * count * second_all - 2.0 * first_all)
        / (count * (count - 1.0))
        / jnp.log(count + 1.0)
    )
    kernel = jnp.exp(-dist / width)
    total = jnp.sum(kernel, axis=1)
    target = 0.5 * width * whole_grads - whole_coords
    pulled = jnp.dot(
        kernel, target, precision=lax.Precision.HIGHEST, preferred_element_type=jnp.float32
    )
    return 2.0 * coords + pulled / total[:, None]


def shards(particles, gradient, curvature):
    first_step = stein_step(particles, gradient)
    relinear = gradient - curvature[None, :] * (first_step - particles)
    return stein_step(first_step, relinear)


def solution(mesh):
    in_specs = (P("dom", "sub"), P("dom", "sub"), P("sub"))
    out_specs = P("dom", "sub")
    return jax.shard_map(shards, mesh=mesh, in_specs=in_specs, out_specs=out_specs, check_vma=False)
```

profile of v0, /device:TPU:1, one launch (start us, length us, event | category | flops | bytes accessed | tf_op | source)
XLA Modules:
  0.0 603.6 jit_solution(12484408973812762776)
XLA Ops:
  6.5 0.0 all-gather.5.cloned.1.call-start
  6.5 0.7 all-gather.5.cloned.1.call-update
  7.3 0.0 all-reduce.7.cloned.1.call-start
  7.3 0.0 copy-start.4
  7.3 1.6 multiply_reduce_fusion.5
  9.0 99.9 %all-gather.5.cloned.1.call-done = f32[3072,512]{1,0:T(8,128)} async-done(((f32[96,512]{1,0:T(8,128)}), f32[3072,512]{1,0:T(8,128)}) %all-gather.5.cloned.1.call-update) | async-done | bytes 6291472 | tf_op jit(solution)/shard_map/all_gather | solution.py:21
  108.9 0.0 copy-start.1
  108.9 3.4 multiply_reduce_fusion.1
  112.3 0.0 copy-done.4
  112.3 1.2 copy-done.1
  113.5 7.2 %fusion.6 = f32[96,3072]{1,0:T(8,128)} fusion(f32[96,512]{1,0:T(8,128)S(1)} %copy-done.4, f32[3072,512]{1,0:T(8,128)S(1)} %copy-done.1, f32[3072]{0:T(1024)S(1)} %multiply_reduce_fusion.1, f32[96]{0:T(128)S(1)} %get-tuple-element.8), kind=kOutput, calls=%fused_computation.10 | convolution fusion | flops 1812824064 | bytes 7680384 | tf_op jit(solution)/shard_map/dot_general | solution.py:10
  120.7 0.0 copy-start.6
  120.7 0.0 copy-start.7
  120.7 0.0 all-reduce.7.cloned.1.call-update
  120.7 0.0 all-gather.7.cloned.1.call-start
  120.7 0.7 all-gather.7.cloned.1.call-update
  121.4 0.0 all-gather.9.cloned.1.call-start
  121.5 66.0 %all-reduce.1 = (f32[]{:T(128)}, f32[512]{0:T(512)S(1)}) all-reduce(f32[]{:T(128)} %get-tuple-element.9, f32[512]{0:T(512)S(1)} %get-tuple-element.10), channel_id=1, replica_groups=mesh['dom'=32,'sub'=8] {'dom'}, use_global_device_ids=true, to_apply=%region_4.0 | all-reduce | flops 513 | bytes 4104 | tf_op jit(solution)/shard_map/psum | solution.py:18
  187.5 0.7 multiply_reduce_fusion.7
  188.2 15.2 %all-reduce.3 = (f32[]{:T(128)}, f32[]{:T(128)}) all-reduce(f32[]{:T(128)} %get-tuple-element.13, f32[]{:T(128)} %multiply_reduce_fusion.7), channel_id=1, replica_groups=mesh['dom'=32,'sub'=8] {'sub'}, use_global_device_ids=true, to_apply=%region_5.0 | all-reduce | flops 2 | bytes 16 | tf_op jit(solution)/shard_map/psum | solution.py:25
  204.7 0.0 all-reduce.7.cloned.1.call-done
  204.7 0.0 copy-start.3
  204.7 1.7 fusion.22
  206.4 90.9 %all-gather.7.cloned.1.call-done = f32[3072,512]{1,0:T(8,128)} async-done(((f32[96,512]{1,0:T(8,128)}), f32[3072,512]{1,0:T(8,128)}) %all-gather.7.cloned.1.call-update) | async-done | bytes 6291472 | tf_op jit(solution)/shard_map/all_gather | solution.py:22
  297.3 0.0 copy-done.6
  297.3 0.0 copy-done.7
  297.3 0.0 copy-done.3
  297.3 10.3 %multiply_reduce_fusion.3 = (f32[96]{0:T(128)S(1)}, f32[]{:T(128)}, f32[512]{0:T(512)S(1)}, f32[96,512]{1,0:T(8,128)}, f32[96,512]{1,0:T(8,128)}) fusion(f32[96,512]{1,0:T(8,128)S(1)} %copy-done.6, f32[96,512]{1,0:T(8,128)S(1)} %copy-done.4, f32[512]{0:T(512)S(1)} %copy-done.7, f32[96]{0:T(128)S(1)} %fusion.22, ...), kind=kOutput, calls=%fused_computation.24 | convolution fusion | flops 1816165760 | bytes 14553868 | tf_op jit(solution)/shard_map/dot_general | solution.py:35
  307.6 0.0 copy-start.5
  307.6 0.0 all-gather.9.cloned.1.call-update
  307.6 0.2 all-reduce.9.cloned.1.call-start
  307.9 91.1 %all-gather.9.cloned.1.call-done = f32[3072,512]{1,0:T(8,128)} async-done(((f32[96,512]{1,0:T(8,128)}), f32[3072,512]{1,0:T(8,128)}) %all-gather.9.cloned.1.call-update) | async-done | bytes 6291472 | tf_op jit(solution)/shard_map/all_gather | solution.py:21
  399.0 3.4 multiply_reduce_fusion
  402.4 0.0 copy-done.5
  402.4 1.2 copy-done
  403.6 7.2 %fusion.7 = f32[96,3072]{1,0:T(8,128)} fusion(f32[96,512]{1,0:T(8,128)S(1)} %copy-done.5, f32[3072,512]{1,0:T(8,128)S(1)} %copy-done, f32[3072]{0:T(1024)S(1)} %multiply_reduce_fusion, f32[96]{0:T(128)S(1)} %get-tuple-element.5), kind=kOutput, calls=%fused_computation.11 | convolution fusion | flops 1812824064 | bytes 7680384 | tf_op jit(solution)/shard_map/dot_general | solution.py:10
  410.7 0.0 all-reduce.9.cloned.1.call-update
  410.8 0.0 all-gather.11.cloned.1.call-start
  410.8 0.5 all-gather.11.cloned.1.call-update
  411.3 65.5 %all-reduce = (f32[]{:T(128)}, f32[512]{0:T(512)S(1)}) all-reduce(f32[]{:T(128)} %get-tuple-element.6, f32[512]{0:T(512)S(1)} %get-tuple-element.7), channel_id=1, replica_groups=mesh['dom'=32,'sub'=8] {'dom'}, use_global_device_ids=true, to_apply=%region_15.0 | all-reduce | flops 513 | bytes 4104 | tf_op jit(solution)/shard_map/psum | solution.py:18
  476.9 0.6 multiply_reduce_fusion.6
  477.5 15.6 %all-reduce.2 = (f32[]{:T(128)}, f32[]{:T(128)}) all-reduce(f32[]{:T(128)} %get-tuple-element.11, f32[]{:T(128)} %multiply_reduce_fusion.6), channel_id=1, replica_groups=mesh['dom'=32,'sub'=8] {'sub'}, use_global_device_ids=true, to_apply=%region_16.0 | all-reduce | flops 2 | bytes 16 | tf_op jit(solution)/shard_map/psum | solution.py:25
  494.5 0.0 all-reduce.9.cloned.1.call-done
  494.5 0.0 copy-start.2
  494.5 1.7 fusion.23
  496.2 91.0 %all-gather.11.cloned.1.call-done = f32[3072,512]{1,0:T(8,128)} async-done(((f32[96,512]{1,0:T(8,128)}), f32[3072,512]{1,0:T(8,128)}) %all-gather.11.cloned.1.call-update) | async-done | bytes 6291472 | tf_op jit(solution)/shard_map/all_gather | solution.py:22
  587.2 0.0 copy-done.2
  587.2 9.6 %fusion.19 = f32[96,512]{1,0:T(8,128)} fusion(f32[3072,512]{1,0:T(8,128)} %all-gather.9.cloned.1.call-done, f32[3072,512]{1,0:T(8,128)} %all-gather.11.cloned.1.call-done, f32[]{:T(128)S(6)} %mul.87, f32[96,3072]{1,0:T(8,128)S(1)} %copy-done.2, f32[]{:T(128)S(6)} %div.41, f32[96,512]{1,0:T(8,128)S(1)} %copy-done.5, f32[96]{0:T(128)S(1)} %fusion.23), kind=kOutput, calls=%fused_computation.19 | convolution fusion | flops 1815822336 | bytes 14156168 | tf_op jit(solution)/shard_map/dot_general | solution.py:35
  (1 shorter events, 0.0 us)
Async XLA Ops:
  6.5 102.4 %all-gather.5.cloned.1.call-start = ((), (), s32[]{:S(2)}) async-start(), calls=%async_computation | async-start | bytes 6488064 | tf_op jit(solution)/shard_map/all_gather | solution.py:21
  7.3 197.4 %all-reduce.7.cloned.1.call-start = ((), (), s32[]{:S(2)}) async-start(), calls=%async_computation.1 | async-start | bytes 2359296 | tf_op jit(solution)/shard_map/psum | solution.py:26
  7.3 105.0 %copy-start.4 = (f32[96,512]{1,0:T(8,128)S(1)}, f32[96,512]{1,0:T(8,128)}, u32[]{:S(2)}) copy-start(f32[96,512]{1,0:T(8,128)} %param.3) | copy-start | bytes 589828
  108.9 4.6 copy-start.1
  120.7 176.6 %copy-start.6 = (f32[96,512]{1,0:T(8,128)S(1)}, f32[96,512]{1,0:T(8,128)}, u32[]{:S(2)}) copy-start(f32[96,512]{1,0:T(8,128)} %param.4) | copy-start | bytes 589828
  120.7 176.6 %copy-start.7 = (f32[512]{0:T(512)S(1)}, f32[512]{0:T(512)}, u32[]{:S(2)}) copy-start(f32[512]{0:T(512)} %param.5) | copy-start | bytes 6148
  120.7 176.6 %all-gather.7.cloned.1.call-start = ((), (), s32[]{:S(2)}) async-start(), calls=%async_computation.2 | async-start | bytes 6488064 | tf_op jit(solution)/shard_map/all_gather | solution.py:22
  121.4 277.5 %all-gather.9.cloned.1.call-start = ((), (), s32[]{:S(2)}) async-start(), calls=%async_computation.3 | async-start | bytes 6488064 | tf_op jit(solution)/shard_map/all_gather | solution.py:21
  204.7 92.6 %copy-start.3 = (f32[96,3072]{1,0:T(8,128)S(1)}, f32[96,3072]{1,0:T(8,128)}, u32[]{:S(2)}) copy-start(f32[96,3072]{1,0:T(8,128)} %all-reduce.7.cloned.1.call-done) | copy-start | bytes 3538948
  307.6 94.8 %copy-start.5 = (f32[96,512]{1,0:T(8,128)S(1)}, f32[96,512]{1,0:T(8,128)}, u32[]{:S(2)}) copy-start(f32[96,512]{1,0:T(8,128)} %get-tuple-element.20) | copy-start | bytes 589828
  307.6 186.9 %all-reduce.9.cloned.1.call-start = ((), (), s32[]{:S(2)}) async-start(), calls=%async_computation.4 | async-start | bytes 2359296 | tf_op jit(solution)/shard_map/psum | solution.py:26
  399.0 4.6 copy-start
  410.8 176.5 %all-gather.11.cloned.1.call-start = ((), (), s32[]{:S(2)}) async-start(), calls=%async_computation.5 | async-start | bytes 6488064 | tf_op jit(solution)/shard_map/all_gather | solution.py:22
  494.5 92.7 %copy-start.2 = (f32[96,3072]{1,0:T(8,128)S(1)}, f32[96,3072]{1,0:T(8,128)}, u32[]{:S(2)}) copy-start(f32[96,3072]{1,0:T(8,128)} %all-reduce.9.cloned.1.call-done) | copy-start | bytes 3538948
Sparse Core Ops, SparseCore 0:
  10.1 98.7 all-gather.4
  120.8 74.2 all-reduce.6
  197.8 99.3 all-gather.6
  307.8 91.1 all-gather.8
  410.9 74.0 all-reduce.8
  487.6 99.5 all-gather.10
where the time goes:
time: 604 us
  waiting for transfers between devices  375 us (62%)
  blocking collectives  162 us (27%)
  matrix products  34.2 us (6%)
  between operations  16.2 us (3%)
  other arithmetic  13.1 us (2%)
    all_gather x2, waiting for transfers between devices, stein_step(): lax.all_gather(coords, 'dom', axis=0, tiled=True)  191 us
    all_gather x2, waiting for transfers between devices, stein_step(): lax.all_gather(grads, 'dom', axis=0, tiled=True)  182 us
    psum x2, blocking collectives, stein_step(): lax.psum((jnp.sum(coords, axis=0), jnp.sum(coords * coords)), 'dom')  132 us
    psum x2, blocking collectives, stein_step(): second_all, first_all = lax.psum((second, first_sq), 'sub')  30.8 us
    dot_general x2, matrix products, stein_step(): jnp.dot(kernel, target, precision=lax.Precision.HIGHEST, preferred_elemen...  19.9 us
    dot_general x2, matrix products, pair_part(): jnp.dot(local, piece.T, precision=lax.Precision.HIGHEST, preferred_elemen...  14.3 us
  transfers between devices with their start and end apart: 6, of which 4 were waited for; matrix products, arithmetic and copies ran while one was open for 1% of the time, Pallas kernels for 0%

commit v1 on v0

v1 whole, which is shorter than its diff:
```python
import functools
import math

import jax
import jax.numpy as jnp
from jax import lax
from jax.experimental import pallas as pl
from jax.experimental.pallas import tpu as pltpu
from jax.sharding import PartitionSpec as P

F32, BF16 = jnp.float32, jnp.bfloat16
MESH = pl.DeviceIdType.MESH
NT = (((1,), (1,)), ((), ()))
TN = (((0,), (0,)), ((), ()))

GROUPS = ((1, 7), (2, 6), (3, 5), (0, 4))
SUBS = tuple((dx, dy) for dx in range(2) for dy in range(4))[1:]
CHUNKS = 4


def split(a):
    high = a.astype(BF16)
    return high, (a - high.astype(F32)).astype(BF16)


def dot3(a, b, dims):
    (ah, al), (bh, bl) = a, b
    dot = functools.partial(lax.dot_general, dimension_numbers=dims, preferred_element_type=F32)
    return dot(al, bh) + dot(ah, bl) + dot(ah, bh)


def copy_to(src, dst, send, recv, device):
    return pltpu.make_async_remote_copy(
        src_ref=src, dst_ref=dst, send_sem=send, recv_sem=recv, device_id=device, device_id_type=MESH
    )


def wait_bytes(ref, sem):
    pltpu.make_async_copy(ref, ref, sem).wait()


class Ring:
    def __init__(self, own, held, send, recv, right, left, by_columns):
        self.own, self.held, self.send, self.recv = own, held, send, recv
        self.to = (right, left)
        self.by_columns = by_columns

    def piece(self, d, chunk):
        ref = self.own if d == 0 else self.held.at[d]
        rows, columns = ref.shape
        if self.by_columns:
            width = columns // CHUNKS
            return ref.at[:, pl.ds(chunk * width, width)]
        height = rows // CHUNKS
        return ref.at[pl.ds(chunk * height, height)]

    def has(self, way, step, chunk):
        return step < 3 or (step == 3 and (chunk % 2 == way))

    def copy(self, way, step, chunk):
        src = (-step) % 8 if way == 0 else step
        dst = (-step - 1) % 8 if way == 0 else step + 1
        return copy_to(
            self.piece(src, chunk), self.piece(dst, chunk), self.send.at[way, step], self.recv.at[way, step, chunk],
            self.to[way],
        )

    def advance(self, step, chunk):
        for way in range(2):
            if step > 0 and self.has(way, step - 1, chunk):
                self.copy(way, step - 1, chunk).wait_recv()
            if self.has(way, step, chunk):
                self.copy(way, step, chunk).start()

    def drain(self):
        for way in range(2):
            for step in range(4):
                ref = self.own if step < 3 else self.own.at[pl.ds(0, self.own.shape[0] // 2)]
                wait_bytes(ref, self.send.at[way, step])


def kernel(
    x_ref, g_ref, c_ref, o_ref,
    x1_ref, held0, held1, heldg, xj, jh, jl, part, dist, rs_recv, kh, kl, th, tl,
    sums, sums_recv, scal, scal_recv, pull, sib_recv, half_send, half_recv,
    ring_send, ring_recv, xj_send, xj_recv, rs_ssem, rs_rsem, ag_ssem, ag_rsem,
    s_ssem, s_rsem, p_ssem, p_rsem,
):
    rows, cols = x_ref.shape
    dom, sub = lax.axis_index("dom"), lax.axis_index("sub")
    core, z, half = dom % 2, (dom // 2) % 8, dom // 16
    y, pair = sub % 4, sub // 4
    count = 1.0 * rows * lax.axis_size("dom")
    piece = 2 * rows // 8
    mine = pl.ds(pl.multiple_of(sub * piece, 8), piece)

    def at(dh, dz, dc):
        return (((half + dh) % 2 * 8 + (z + dz) % 8) * 2 + (core + dc) % 2, sub)

    def sub_index(dx, dy):
        return (pair + dx) % 2 * 4 + (y + dy) % 4

    right, left, sibling, other, cross = at(0, 1, 0), at(0, 7, 0), at(0, 0, 1), at(1, 0, 0), at(1, 0, 1)
    subs = [(dom, sub_index(dx, dy)) for dx, dy in SUBS]

    barrier = pltpu.get_barrier_semaphore()
    partners = [right, left, sibling, other, cross] + subs
    for partner in partners:
        pl.semaphore_signal(barrier, inc=1, device_id=partner, device_id_type=MESH)
    pl.semaphore_wait(barrier, len(partners))

    ring_g = Ring(g_ref, heldg, ring_send.at[2], ring_recv.at[2], right, left, True)

    def stein(s, own, held, make_target, out):
        ring = Ring(own, held, ring_send.at[s], ring_recv.at[s], right, left, False)

        def block(d):
            return own[...] if d == 0 else held[d]

        def xj_copy(k, chunk):
            rows_of = pl.ds(chunk * (rows // 2), rows // 2)
            src = own if k < 3 else xj.at[s, 2]
            return copy_to(
                src.at[rows_of], xj.at[s, k, rows_of], xj_send.at[s, k, chunk], xj_recv.at[s, k, chunk],
                other if k == 2 else sibling,
            )

        for chunk in range(2):
            xj_copy(2, chunk).start()
        for chunk in range(CHUNKS):
            ring.advance(0, chunk)
        for chunk in range(2):
            xj_copy(1, chunk).start()
        for chunk in range(CHUNKS):
            ring.advance(1, chunk)

        for chunk in range(2):
            xj_copy(2, chunk).wait_recv()
            xj_copy(3, chunk).start()
        xj[s, 0] = own[...]
        for chunk in range(2):
            xj_copy(1, chunk).wait_recv()
        for chunk in range(2):
            xj_copy(3, chunk).wait_recv()
        js = xj[s].reshape(4 * rows, cols)
        jh[...], jl[...] = split(-2.0 * js)
        norms_j = lax.dot_general(
            jnp.ones((8, cols), F32), js * js, NT, precision=lax.Precision.HIGHEST, preferred_element_type=F32
        )[0:1]

        def rs_copy(g, i):
            where = pl.ds(pl.multiple_of(sub_index(*SUBS[i]) * piece, 8), piece)
            return copy_to(part.at[s, g, where], rs_recv.at[s, g, i], rs_ssem.at[s, g], rs_rsem.at[s, g], subs[i])

        def ag_copy(g, i):
            return copy_to(dist.at[s, g, mine], dist.at[s, g, mine], ag_ssem.at[s, g], ag_rsem.at[s, g], subs[i])

        def gram(g):
            a = jnp.concatenate([block(d) for d in GROUPS[g]], axis=0)
            norms = jnp.sum(a * a, axis=1, keepdims=True)
            part[s, g] = dot3(split(a), (jh[...], jl[...]), NT) + norms + norms_j
            for i in range(7):
                rs_copy(g, i).start()

        def add_up(g):
            wait_bytes(rs_recv.at[s, g], rs_rsem.at[s, g])
            total = part[s, g, mine]
            for i in range(7):
                total = total + rs_recv[s, g, i]
            dist[s, g, mine] = total
            for i in range(7):
                ag_copy(g, i).start()

        gram(0)
        for chunk in range(CHUNKS):
            ring.advance(2, chunk)
        gram(1)
        add_up(0)
        for chunk in range(CHUNKS):
            ring.advance(3, chunk)
        if s == 0:
            for chunk in range(2):
                ring_g.advance(0, chunk)
        gram(2)
        add_up(1)
        for chunk in range(CHUNKS):
            ring.advance(4, chunk)
        gram(3)

        first = jnp.zeros((8, cols), F32)
        second = jnp.zeros((8, cols), F32)
        for d in range(8):
            b = block(d).reshape(rows // 8, 8, cols)
            first = first + jnp.sum(b, axis=0)
            second = second + jnp.sum(b * b, axis=0)
        sums[s, 0], sums[s, 1] = first, second

        def sums_copy(i):
            return copy_to(
                sums.at[s], sums_recv.at[s, i], s_ssem.at[s, 0], s_rsem.at[s, 0], (sibling, other, cross)[i]
            )

        def scal_copy(i):
            return copy_to(scal.at[s], scal_recv.at[s, i], s_ssem.at[s, 1], s_rsem.at[s, 1], subs[i])

        for i in range(3):
            sums_copy(i).start()
        if s == 0:
            for chunk in range(2):
                ring_g.advance(1, chunk)
        add_up(2)
        wait_bytes(sums_recv.at[s], s_rsem.at[s, 0])
        both = sums[s] + sums_recv[s, 0] + sums_recv[s, 1] + sums_recv[s, 2]
        first = jnp.sum(both[0], axis=0, keepdims=True)
        scal[s, 0] = jnp.broadcast_to(first * first, (8, cols))
        scal[s, 1] = both[1]
        for i in range(7):
            scal_copy(i).start()
        if s == 0:
            for chunk in range(2):
                ring_g.advance(2, chunk)
        add_up(3)
        if s == 0:
            for chunk in range(2):
                ring_g.advance(3, chunk)
            for chunk in range(2, 4):
                ring_g.advance(0, chunk)
        wait_bytes(scal_recv.at[s], s_rsem.at[s, 1])
        both = scal[s]
        for i in range(7):
            both = both + scal_recv[s, i]
        first_sq = jnp.sum(both[0, 0:1], axis=1, keepdims=True)
        second_all = jnp.sum(jnp.sum(both[1], axis=0, keepdims=True), axis=1, keepdims=True)
        width = (2.0 * count * second_all - 2.0 * first_sq) / (count * (count - 1.0)) / math.log(count + 1.0)

        def weights(g):
            wait_bytes(dist.at[s, g, pl.ds(0, 7 * piece)], ag_rsem.at[s, g])
            k = jnp.exp(-dist[s, g] / width)
            where = pl.ds(g * 2 * rows, 2 * rows)
            kh[where], kl[where] = split(k)

        def h_copy(part_of):
            return copy_to(
                half_send.at[s, part_of], half_recv.at[s, part_of], p_ssem.at[s, part_of, 2],
                p_rsem.at[s, part_of, 2], other,
            )

        def target(part_of):
            width_of = cols // 2
            lanes = pl.ds(part_of * width_of, width_of)
            for g in range(4):
                for e, d in enumerate(GROUPS[g]):
                    where = pl.ds((2 * g + e) * rows, rows)
                    th[where, lanes], tl[where, lanes] = split(make_target(d, lanes, width))

        def pulled(part_of):
            width_of = cols // 2
            lanes = pl.ds(part_of * width_of, width_of)
            result = dot3((kh[...], kl[...]), (th[:, lanes], tl[:, lanes]), TN)
            pull_s[part_of, :, :, 0:width_of] = result.reshape(4, rows, width_of)
            for side in range(2):
                p_copy(part_of, side).start()

        def across(part_of):
            p_copy(part_of, 1).wait_recv()
            half_send[s, part_of] = pull_s[part_of, 2] + sib_recv[s, part_of, 1]
            h_copy(part_of).start()

        def finish(part_of):
            p_copy(part_of, 0).wait_recv()
            h_copy(part_of).wait_recv()
            return pull_s[part_of, 0] + sib_recv[s, part_of, 0] + half_recv[s, part_of]

        pull_s = pull.at[s]

        def p_copy(part_of, side):
            return copy_to(
                pull_s.at[part_of, 1 + 2 * side], sib_recv.at[s, part_of, side], p_ssem.at[s, part_of, side],
                p_rsem.at[s, part_of, side], sibling,
            )

        weights(0)
        if s == 0:
            for chunk in range(2):
                ring_g.advance(4, chunk)
            for chunk in range(2, 4):
                ring_g.advance(1, chunk)
        weights(1)
        target(0)
        if s == 0:
            for chunk in range(2, 4):
                ring_g.advance(2, chunk)
        weights(2)
        if s == 0:
            for chunk in range(2, 4):
                ring_g.advance(3, chunk)
        weights(3)
        ones = jnp.ones((8 * rows, 128), BF16)
        dot = functools.partial(lax.dot_general, dimension_numbers=TN, preferred_element_type=F32)
        pull_s[0, :, :, cols // 2 :] = (dot(kl[...], ones) + dot(kh[...], ones)).reshape(4, rows, 128)
        pull_s[1, :, :, cols // 2 :] = jnp.zeros((4, rows, 128), F32)
        pulled(0)
        if s == 0:
            for chunk in range(2, 4):
                ring_g.advance(4, chunk)
        target(1)
        across(0)
        pulled(1)
        across(1)
        whole = finish(0)
        total = whole[:, cols // 2 : cols // 2 + 1]
        out[:, 0 : cols // 2] = 2.0 * own[:, 0 : cols // 2] + whole[:, 0 : cols // 2] / total
        whole = finish(1)
        out[:, cols // 2 :] = 2.0 * own[:, cols // 2 :] + whole[:, 0 : cols // 2] / total

        def drain():
            ring.drain()
            for k in range(1, 4):
                for chunk in range(2):
                    xj_copy(k, chunk).wait_send()
            for g in range(4):
                wait_bytes(part.at[s, g, pl.ds(0, 7 * piece)], rs_ssem.at[s, g])
                wait_bytes(part.at[s, g, pl.ds(0, 7 * piece)], ag_ssem.at[s, g])
            wait_bytes(sums_recv.at[s], s_ssem.at[s, 0])
            wait_bytes(scal_recv.at[s], s_ssem.at[s, 1])
            for part_of in range(2):
                for side in range(2):
                    p_copy(part_of, side).wait_send()
                h_copy(part_of).wait_send()

        return drain

    def target0(d, lanes, width):
        x = x_ref[:, lanes] if d == 0 else held0[d, :, lanes]
        g = g_ref[:, lanes] if d == 0 else heldg[d, :, lanes]
        return 0.5 * width * g - x

    def target1(d, lanes, width):
        x0 = x_ref[:, lanes] if d == 0 else held0[d, :, lanes]
        g = g_ref[:, lanes] if d == 0 else heldg[d, :, lanes]
        x = x1_ref[:, lanes] if d == 0 else held1[d, :, lanes]
        return 0.5 * width * (g - c_ref[0:1, lanes] * (x - x0)) - x

    drains = [stein(0, x_ref, held0, target0, x1_ref)]
    drains.append(stein(1, x1_ref, held1, target1, o_ref))
    for drain in drains:
        drain()
    ring_g.drain()


def shards(particles, gradient, curvature):
    rows, cols = particles.shape
    lanes_j = 4 * rows
    piece = 2 * rows // 8
    wide = cols // 2 + 128
    vmem = pl.BlockSpec(memory_space=pltpu.VMEM)
    dma = pltpu.SemaphoreType.DMA
    return pl.pallas_call(
        kernel,
        name="stein",
        out_shape=jax.ShapeDtypeStruct((rows, cols), F32),
        in_specs=[vmem] * 3,
        out_specs=vmem,
        scratch_shapes=[
            pltpu.VMEM((rows, cols), F32),
            pltpu.VMEM((8, rows, cols), F32),
            pltpu.VMEM((8, rows, cols), F32),
            pltpu.VMEM((8, rows, cols), F32),
            pltpu.VMEM((2, 4, rows, cols), F32),
            pltpu.VMEM((lanes_j, cols), BF16),
            pltpu.VMEM((lanes_j, cols), BF16),
            pltpu.VMEM((2, 4, 2 * rows, lanes_j), F32),
            pltpu.VMEM((2, 4, 2 * rows, lanes_j), F32),
            pltpu.VMEM((2, 4, 7, piece, lanes_j), F32),
            pltpu.VMEM((8 * rows, lanes_j), BF16),
            pltpu.VMEM((8 * rows, lanes_j), BF16),
            pltpu.VMEM((8 * rows, cols), BF16),
            pltpu.VMEM((8 * rows, cols), BF16),
            pltpu.VMEM((2, 2, 8, cols), F32),
            pltpu.VMEM((2, 3, 2, 8, cols), F32),
            pltpu.VMEM((2, 2, 8, cols), F32),
            pltpu.VMEM((2, 7, 2, 8, cols), F32),
            pltpu.VMEM((2, 2, 4, rows, wide), F32),
            pltpu.VMEM((2, 2, 2, rows, wide), F32),
            pltpu.VMEM((2, 2, rows, wide), F32),
            pltpu.VMEM((2, 2, rows, wide), F32),
            dma((3, 2, 4)),
            dma((3, 2, 4, CHUNKS)),
            dma((2, 4, 2)),
            dma((2, 4, 2)),
            dma((2, 4)),
            dma((2, 4)),
            dma((2, 4)),
            dma((2, 4)),
            dma((2, 2)),
            dma((2, 2)),
            dma((2, 2, 3)),
            dma((2, 2, 3)),
        ],
        compiler_params=pltpu.CompilerParams(
            collective_id=0, has_side_effects=True, vmem_limit_bytes=52 * 2**20
        ),
    )(particles, gradient, curvature.reshape(1, cols))


def solution(mesh):
    in_specs = (P("dom", "sub"), P("dom", "sub"), P("sub"))
    out_specs = P("dom", "sub")
    return jax.shard_map(shards, mesh=mesh, in_specs=in_specs, out_specs=out_specs, check_vma=False)
```

time: 604 us -> 130 us (0.22)
  waiting for transfers between devices: 375 us -> 0 us
  blocking collectives: 162 us -> 0 us
  Pallas kernels: 0 us -> 127 us
  matrix products: 34.2 us -> 0 us
  between operations: 16.2 us -> 0.01 us
  other arithmetic: 13.1 us -> 0 us
    all_gather x4 -> x0, waiting for transfers between devices: 373 us -> none  [the longest x2 191 us: stein_step(): lax.all_gather(coords, 'dom', axis=0, tiled=True)]
    psum x4 -> x0, blocking collectives: 162 us -> none  [the longest x2 132 us: stein_step(): lax.psum((jnp.sum(coords, axis=0), jnp.sum(coords * coords)), 'dom')]
    pallas_call x0 -> x1, Pallas kernels: none -> 127 us  [shards(): pl.pallas_call(kernel, name='stein', out_shape=jax.ShapeDtypeStruct((rows...]
    dot_general x4 -> x0, matrix products: 34.2 us -> none  [the longest x2 19.9 us: stein_step(): jnp.dot(kernel, target, precision=lax.Precision.HIGHEST, preferred_elemen...]
    reduce_sum x7 -> x0, other arithmetic: 13.1 us -> none  [the longest x2 6.85 us: pair_part(): piece_norms = jnp.sum(piece * piece, axis=1)]
  transfers between devices with their start and end apart: 6 -> 0, of which waited for: 4 -> 0; matrix products, arithmetic and copies ran while one was open for 1% -> 0% of each run, Pallas kernels for 0% -> 0%
where the time goes in v1:
time: 130 us
  Pallas kernels  127 us (98%)
  local copies, waits for them, and re-layouts  3.21 us (2%)
    pallas_call x1, Pallas kernels, shards(): pl.pallas_call(kernel, name='stein', out_shape=jax.ShapeDtypeStruct((rows...  127 us
    unnamed x7, local copies, waits for them, and re-layouts  3.21 us

profile of v1, /device:TPU:1, one launch (start us, length us, event | category | flops | bytes accessed | tf_op | source)
XLA Modules:
  0.0 130.2 jit_solution(12588639953282762051)
XLA Ops:
  0.0 0.0 copy-start
  0.0 0.9 copy-done
  0.9 0.0 copy-start.1
  0.9 0.9 copy-done.1
  1.9 0.0 copy-start.2
  1.9 0.7 copy-done.2
  2.5 127.0 %stein.1 = f32[96,512]{1,0:T(8,128)S(1)} custom-call(f32[96,512]{1,0:T(8,128)S(1)} %copy-done, f32[96,512]{1,0:T(8,128)S(1)} %copy-done.1, f32[1,512]{1,0:T(1,128)S(1)} %bitcast.1), custom_call_target="tpu_custom_call" | custom-call | tf_op jit(solution)/shard_map/stein/pallas_call | solution.py:358
  129.5 0.7 copy.5
Async XLA Ops:
  0.0 0.9 copy-start
  0.9 0.9 copy-start.1
  1.9 0.7 copy-start.2

commit v2 on v0

v2 whole, which is shorter than its diff:
```python
import functools
import math

import jax
import jax.numpy as jnp
from jax import lax
from jax.experimental import pallas as pl
from jax.experimental.pallas import tpu as pltpu
from jax.sharding import PartitionSpec as P

F32, BF16 = jnp.float32, jnp.bfloat16
MESH = pl.DeviceIdType.MESH
NT = (((1,), (1,)), ((), ()))
NN = (((1,), (0,)), ((), ()))

GROUPS = ((1, 7), (2, 6), (3, 5), (0, 4))
SUBS = tuple((dx, dy) for dx in range(2) for dy in range(4))[1:]
CHUNKS = 4


def split(a):
    high = a.astype(BF16)
    return high, (a - high.astype(F32)).astype(BF16)


def dot3(a, b, dims):
    (ah, al), (bh, bl) = a, b
    dot = functools.partial(lax.dot_general, dimension_numbers=dims, preferred_element_type=F32)
    return dot(al, bh) + dot(ah, bl) + dot(ah, bh)


def copy_to(src, dst, send, recv, device):
    return pltpu.make_async_remote_copy(
        src_ref=src, dst_ref=dst, send_sem=send, recv_sem=recv, device_id=device, device_id_type=MESH
    )


def wait_bytes(ref, sem):
    pltpu.make_async_copy(ref, ref, sem).wait()


class Ring:
    def __init__(self, held, send, recv, sib_send, sib_recv, right, left, sibling):
        self.held, self.send, self.recv = held, send, recv
        self.sib_send, self.sib_recv = sib_send, sib_recv
        self.to, self.sibling = (right, left), sibling

    def piece(self, d, chunk):
        width = self.held.shape[3] // CHUNKS
        return self.held.at[0, d, :, pl.ds(chunk * width, width)]

    def has(self, way, step, chunk):
        return step < 3 or (step == 3 and (chunk % 2 == way))

    def copy(self, way, step, chunk):
        src = (-step) % 8 if way == 0 else step
        dst = (-step - 1) % 8 if way == 0 else step + 1
        return copy_to(
            self.piece(src, chunk), self.piece(dst, chunk), self.send.at[way, step], self.recv.at[way, step, chunk],
            self.to[way],
        )

    def advance(self, step, chunks=range(CHUNKS)):
        for chunk in chunks:
            for way in range(2):
                if step > 0 and self.has(way, step - 1, chunk):
                    self.copy(way, step - 1, chunk).wait_recv()
                if self.has(way, step, chunk):
                    self.copy(way, step, chunk).start()

    def sib_copy(self, d):
        return copy_to(self.held.at[0, d], self.held.at[1, d], self.sib_send.at[d], self.sib_recv.at[d], self.sibling)

    def hand(self, *blocks):
        for d in blocks:
            self.sib_copy(d).start()

    def wait_handed(self, *blocks):
        for d in blocks:
            self.sib_copy(d).wait_recv()

    def drain(self):
        block = self.held.at[0, 0]
        for way in range(2):
            for step in range(4):
                ref = block if step < 3 else block.at[pl.ds(0, block.shape[0] // 2)]
                wait_bytes(ref, self.send.at[way, step])
        for d in range(8):
            self.sib_copy(d).wait_send()


def kernel(
    x_ref, g_ref, c_ref, o_ref,
    hx, hg, cv, xo, jx, jh, jl, part, dist, rs_recv, th, tl, pull, p_recv, tot, t_send, t_recv,
    jsum, jsum_recv, zsum, zsum_recv, scal, scal_recv,
    ring_send, ring_recv, sib_send, sib_recv, xo_send, xo_recv, rs_ssem, rs_rsem, ag_ssem, ag_rsem,
    s_ssem, s_rsem, p_ssem, p_rsem, in_sem,
):
    rows, cols = o_ref.shape
    dom, sub = lax.axis_index("dom"), lax.axis_index("sub")
    core, z, half = dom % 2, (dom // 2) % 8, dom // 16
    y, pair = sub % 4, sub // 4
    count = 1.0 * rows * lax.axis_size("dom")
    piece = 2 * rows // 8
    mine = pl.ds(pl.multiple_of(sub * piece, 8), piece)
    own_rows = pl.ds(pl.multiple_of(core * rows, 16), rows)
    other_rows = pl.ds(pl.multiple_of((1 - core) * rows, 16), rows)
    adds_other = (pair + core) % 2

    def at(dh, dz, dc):
        return (((half + dh) % 2 * 8 + (z + dz) % 8) * 2 + (core + dc) % 2, sub)

    def sub_index(dx, dy):
        return (pair + dx) % 2 * 4 + (y + dy) % 4

    zs = [at(0, dz, 0) for dz in range(1, 8)]
    right, left, sibling, other = zs[0], zs[6], at(0, 0, 1), at(1, 0, 0)
    sub_at = [sub_index(dx, dy) for dx, dy in SUBS]
    subs = [(dom, i) for i in sub_at]

    moves = [
        pltpu.make_async_copy(src, dst, in_sem.at[i])
        for i, (src, dst) in enumerate(((x_ref, hx.at[0, 0, 0]), (g_ref, hg.at[0, 0]), (c_ref, cv)))
    ]
    for move in moves:
        move.start()
    barrier = pltpu.get_barrier_semaphore()
    partners = zs + [sibling, other] + subs
    for partner in partners:
        pl.semaphore_signal(barrier, inc=1, device_id=partner, device_id_type=MESH)
    for move in moves:
        move.wait()
    pl.semaphore_wait(barrier, len(partners))

    def ring_of(i, held):
        return Ring(
            held, ring_send.at[i], ring_recv.at[i], sib_send.at[i], sib_recv.at[i], right, left, sibling
        )

    rings = [ring_of(0, hx.at[0]), ring_of(1, hx.at[1])]
    ring_g = ring_of(2, hg)

    def lanes_of(hf):
        return pl.ds(hf * (cols // 2), cols // 2)

    def xo_copy(s, hf):
        return copy_to(
            hx.at[s, 0, 0, :, lanes_of(hf)], xo.at[s, :, lanes_of(hf)], xo_send.at[s, hf], xo_recv.at[s, hf], other
        )

    def begin(s, hf):
        xo_copy(s, hf).start()
        rings[s].advance(0, (2 * hf, 2 * hf + 1))

    def stein(s):
        ring = rings[s]

        def rs_copy(g, i):
            where = pl.ds(pl.multiple_of(sub_at[i] * piece, 8), piece)
            return copy_to(part.at[s, g, where], rs_recv.at[s, g, i], rs_ssem.at[s, g], rs_rsem.at[s, g], subs[i])

        def ag_copy(g, i):
            return copy_to(
                dist.at[s, g, mine], dist.at[s, g, mine], ag_ssem.at[s, g], ag_rsem.at[s, g, SUBS[i][0]], subs[i]
            )

        def members(g):
            return [(d, e) for d in GROUPS[g] for e in range(2)]

        def gram(g):
            a = jnp.concatenate([hx[s, e, d] for d, e in members(g)], axis=0)
            norms = jnp.sum(a * a, axis=1, keepdims=True)
            norms = jnp.broadcast_to(norms, (a.shape[0], 128)).T[0:1]
            part[s, g] = dot3((jh[...], jl[...]), split(a), NT) + norms_j + norms
            for i in range(7):
                rs_copy(g, i).start()

        def add_up(g):
            wait_bytes(rs_recv.at[s, g], rs_rsem.at[s, g])
            total = part[s, g, mine]
            for i in range(7):
                total = total + rs_recv[s, g, i]
            dist[s, g, mine] = total
            for i in range(7):
                ag_copy(g, i).start()

        def add_up_if(kind, *groups):
            @pl.when(adds_other == kind)
            def _():
                for g in groups:
                    add_up(g)

        def wait_rows(g, kind):
            @pl.when(adds_other == kind)
            def _():
                wait_bytes(dist.at[s, g, pl.ds(0, 3 * piece)], ag_rsem.at[s, g, 0])

            @pl.when(adds_other != kind)
            def _():
                wait_bytes(dist.at[s, g, pl.ds(0, 4 * piece)], ag_rsem.at[s, g, 1])

        def jsum_copy():
            return copy_to(jsum.at[s], jsum_recv.at[s], s_ssem.at[s, 0], s_rsem.at[s, 0], sibling)

        def zsum_copy(i):
            return copy_to(zsum.at[s], zsum_recv.at[s, i], s_ssem.at[s, 1], s_rsem.at[s, 1], zs[i])

        def scal_copy(i):
            return copy_to(scal.at[s], scal_recv.at[s, i], s_ssem.at[s, 2], s_rsem.at[s, 2], subs[i])

        ring.advance(1)
        ring.hand(1, 7)

        for hf in range(2):
            xo_copy(s, hf).wait_recv()
        jx[own_rows] = hx[s, 0, 0]
        jx[other_rows] = xo[s]
        js = jx[...]
        jh[...], jl[...] = split(-2.0 * js)
        squares = js * js
        norms_j = jnp.sum(squares, axis=1, keepdims=True)
        sums = [jnp.sum(a, axis=0, keepdims=True) for a in (js, squares)]
        jsum[s] = jnp.concatenate([a[:, k * 128 : k * 128 + 128] for a in sums for k in range(4)], axis=0)
        jsum_copy().start()

        ring.advance(2, (0, 1))
        ring.wait_handed(1, 7)
        gram(0)
        jsum_copy().wait_recv()
        zsum[s] = jsum[s] + jsum_recv[s]
        for i in range(7):
            zsum_copy(i).start()
        ring.advance(2, (2, 3))
        ring.hand(2, 6)
        ring.advance(3, (0,))
        ring.wait_handed(2, 6)
        gram(1)
        ring.advance(3, (1,))
        add_up_if(1, 0)
        ring.advance(3, (2, 3))
        ring.hand(3, 5)
        if s == 0:
            ring_g.advance(0)
            ring_g.hand(0)
        ring.wait_handed(3, 5)
        gram(2)
        ring.advance(4)
        ring.hand(4)
        add_up_if(1, 1)
        wait_bytes(zsum_recv.at[s], s_rsem.at[s, 1])
        both = zsum[s]
        for i in range(7):
            both = both + zsum_recv[s, i]
        scal[s, 0:4] = both[0:4] * both[0:4]
        scal[s, 4:8] = both[4:8]
        for i in range(7):
            scal_copy(i).start()
        ring.wait_handed(0, 4)
        gram(3)
        if s == 0:
            ring_g.advance(1)
            ring_g.hand(1, 7)
        add_up_if(1, 2)
        if s == 0:
            ring_g.advance(2)
            ring_g.hand(2, 6)
        add_up_if(1, 3)
        add_up_if(0, 0, 1, 2, 3)
        wait_bytes(scal_recv.at[s], s_rsem.at[s, 2])
        both = scal[s]
        for i in range(7):
            both = both + scal_recv[s, i]
        both = jnp.sum(both, axis=1, keepdims=True)
        first_sq = jnp.sum(both[0:4], axis=0, keepdims=True)
        second_all = jnp.sum(both[4:8], axis=0, keepdims=True)
        width = (2.0 * count * second_all - 2.0 * first_sq) / (count * (count - 1.0)) / math.log(count + 1.0)

        whole = pl.ds(0, cols)

        def target(d, e, lanes):
            x, g = hx[s, e, d, :, lanes], hg[e, d, :, lanes]
            if s == 1:
                g = g - cv[0:1, lanes] * (x - hx[0, e, d, :, lanes])
            return 0.5 * width * g - x

        def targets(g):
            t = jnp.concatenate([target(d, e, whole) for d, e in members(g)], axis=0)
            th[g], tl[g] = split(t)

        def weights(g, kind):
            wait_rows(g, kind)
            k = jnp.exp(-dist[s, g, other_rows if kind else own_rows] / width)
            total = jnp.broadcast_to(jnp.sum(k, axis=1, keepdims=True), (rows, 128))
            tot[kind, 128 - rows :] = total if g == 0 else tot[kind, 128 - rows :] + total
            return split(k)

        def pulled(g, kind, k, lanes):
            where = other_rows if kind else own_rows
            result = dot3(k, (th[g, :, lanes], tl[g, :, lanes]), NN)
            pull[s, where, lanes] = result if g == 0 else pull[s, where, lanes] + result

        def p_copy(hf):
            return copy_to(
                pull.at[s, other_rows, lanes_of(hf)], p_recv.at[s, :, lanes_of(hf)], p_ssem.at[s, hf],
                p_rsem.at[s, hf], other,
            )

        def t_copy():
            return copy_to(t_send.at[s], t_recv.at[s], p_ssem.at[s, 2], p_rsem.at[s, 2], other)

        tot[1, 0 : 128 - rows] = jnp.zeros((128 - rows, 128), F32)
        for g in range(4):
            if s == 0:
                ring_g.wait_handed(*GROUPS[g])
            if s == 0 and g == 0:
                ring_g.advance(3)
                ring_g.hand(3, 5)
            targets(g)
            k = weights(g, 1)
            if g < 3:
                pulled(g, 1, k, whole)
            if s == 0 and g == 1:
                ring_g.advance(4)
                ring_g.hand(4)
        t_send[s] = tot[1].T[0:8]
        t_copy().start()
        for hf in range(2):
            pulled(3, 1, k, lanes_of(hf))
            p_copy(hf).start()
        for g in range(4):
            pulled(g, 0, weights(g, 0), whole)
        t_copy().wait_recv()
        theirs = jnp.broadcast_to(t_recv[s, 0:1], (128, 128)).T[128 - rows :, 0:1]
        total = tot[0, 128 - rows :, 0:1] + theirs
        for hf in range(2):
            lanes = lanes_of(hf)
            p_copy(hf).wait_recv()
            moved = 2.0 * hx[s, 0, 0, :, lanes] + (pull[s, own_rows, lanes] + p_recv[s, :, lanes]) / total
            if s == 0:
                hx[1, 0, 0, :, lanes] = moved
                begin(1, hf)
            else:
                o_ref[:, lanes] = moved
        if s == 0:
            rings[1].hand(0)

        def drain():
            ring.drain()
            for hf in range(2):
                xo_copy(s, hf).wait_send()
                p_copy(hf).wait_send()
            t_copy().wait_send()
            for g in range(4):
                wait_bytes(part.at[s, g, pl.ds(0, 7 * piece)], rs_ssem.at[s, g])
                wait_bytes(part.at[s, g, pl.ds(0, 7 * piece)], ag_ssem.at[s, g])
            jsum_copy().wait_send()
            wait_bytes(zsum_recv.at[s], s_ssem.at[s, 1])
            wait_bytes(scal_recv.at[s], s_ssem.at[s, 2])

        return drain

    for hf in range(2):
        begin(0, hf)
    rings[0].hand(0)
    drains = [stein(0), stein(1), ring_g.drain]
    for drain in drains:
        drain()


def shards(particles, gradient, curvature):
    rows, cols = particles.shape
    near, far = 2 * rows, 4 * rows
    piece = near // 8
    vmem = pl.BlockSpec(memory_space=pltpu.VMEM)
    dma = pltpu.SemaphoreType.DMA
    return pl.pallas_call(
        kernel,
        name="stein",
        out_shape=jax.ShapeDtypeStruct((rows, cols), F32),
        in_specs=[pl.BlockSpec(memory_space=pltpu.HBM)] * 3,
        out_specs=vmem,
        scratch_shapes=[
            pltpu.VMEM((2, 2, 8, rows, cols), F32),
            pltpu.VMEM((2, 8, rows, cols), F32),
            pltpu.VMEM((1, cols), F32),
            pltpu.VMEM((2, rows, cols), F32),
            pltpu.VMEM((near, cols), F32),
            pltpu.VMEM((near, cols), BF16),
            pltpu.VMEM((near, cols), BF16),
            pltpu.VMEM((2, 4, near, far), F32),
            pltpu.VMEM((2, 4, near, far), F32),
            pltpu.VMEM((2, 4, 7, piece, far), F32),
            pltpu.VMEM((4, far, cols), BF16),
            pltpu.VMEM((4, far, cols), BF16),
            pltpu.VMEM((2, near, cols), F32),
            pltpu.VMEM((2, rows, cols), F32),
            pltpu.VMEM((2, 128, 128), F32),
            pltpu.VMEM((2, 8, 128), F32),
            pltpu.VMEM((2, 8, 128), F32),
            pltpu.VMEM((2, 8, 128), F32),
            pltpu.VMEM((2, 8, 128), F32),
            pltpu.VMEM((2, 8, 128), F32),
            pltpu.VMEM((2, 7, 8, 128), F32),
            pltpu.VMEM((2, 8, 128), F32),
            pltpu.VMEM((2, 7, 8, 128), F32),
            dma((3, 2, 4)),
            dma((3, 2, 4, CHUNKS)),
            dma((3, 8)),
            dma((3, 8)),
            dma((2, 2)),
            dma((2, 2)),
            dma((2, 4)),
            dma((2, 4)),
            dma((2, 4)),
            dma((2, 4, 2)),
            dma((2, 3)),
            dma((2, 3)),
            dma((2, 3)),
            dma((2, 3)),
            dma((3,)),
        ],
        compiler_params=pltpu.CompilerParams(
            collective_id=0, has_side_effects=True, vmem_limit_bytes=63 * 2**20 + 2**19
        ),
    )(particles, gradient, curvature.reshape(1, cols))


def solution(mesh):
    in_specs = (P("dom", "sub"), P("dom", "sub"), P("sub"))
    out_specs = P("dom", "sub")
    return jax.shard_map(shards, mesh=mesh, in_specs=in_specs, out_specs=out_specs, check_vma=False)
```

time: 604 us -> 101 us (0.17)
  waiting for transfers between devices: 375 us -> 0 us
  blocking collectives: 162 us -> 0 us
  Pallas kernels: 0 us -> 99.1 us
  matrix products: 34.2 us -> 0 us
  between operations: 16.2 us -> 0.01 us
  other arithmetic: 13.1 us -> 0 us
    all_gather x4 -> x0, waiting for transfers between devices: 373 us -> none  [the longest x2 191 us: stein_step(): lax.all_gather(coords, 'dom', axis=0, tiled=True)]
    psum x4 -> x0, blocking collectives: 162 us -> none  [the longest x2 132 us: stein_step(): lax.psum((jnp.sum(coords, axis=0), jnp.sum(coords * coords)), 'dom')]
    pallas_call x0 -> x1, Pallas kernels: none -> 99.1 us  [shards(): pl.pallas_call(kernel, name='stein', out_shape=jax.ShapeDtypeStruct((rows...]
    dot_general x4 -> x0, matrix products: 34.2 us -> none  [the longest x2 19.9 us: stein_step(): jnp.dot(kernel, target, precision=lax.Precision.HIGHEST, preferred_elemen...]
    reduce_sum x7 -> x0, other arithmetic: 13.1 us -> none  [the longest x2 6.85 us: pair_part(): piece_norms = jnp.sum(piece * piece, axis=1)]
  transfers between devices with their start and end apart: 6 -> 0, of which waited for: 4 -> 0; matrix products, arithmetic and copies ran while one was open for 1% -> 0% of each run, Pallas kernels for 0% -> 0%
where the time goes in v2:
time: 101 us
  Pallas kernels  99.1 us (98%)
  local copies, waits for them, and re-layouts  1.62 us (2%)
    pallas_call x1, Pallas kernels, shards(): pl.pallas_call(kernel, name='stein', out_shape=jax.ShapeDtypeStruct((rows...  99.1 us

profile of v2, /device:TPU:1, one launch (start us, length us, event | category | flops | bytes accessed | tf_op | source)
XLA Modules:
  0.0 100.7 jit_solution(16565045517861676039)
XLA Ops:
  0.0 99.1 %stein.1 = f32[96,512]{1,0:T(8,128)} custom-call(f32[96,512]{1,0:T(8,128)} %x_ref.1, f32[96,512]{1,0:T(8,128)} %g_ref.1, f32[1,512]{1,0:T(1,128)} %bitcast.1), custom_call_target="tpu_custom_call" | custom-call | tf_op jit(solution)/shard_map/stein/pallas_call | solution.py:376
  99.1 1.6 %copy.5 = f32[96,512]{1,0:T(8,128)} copy(f32[96,512]{1,0:T(8,128)} %stein.1) | data formatting | bytes 393216

commit v3 on v2

--- a/solution.py
+++ b/solution.py
@@ -92,9 +92,9 @@
 def kernel(
     x_ref, g_ref, c_ref, o_ref,
     hx, hg, cv, xo, jx, jh, jl, part, dist, rs_recv, th, tl, pull, p_recv, tot, t_send, t_recv,
-    jsum, jsum_recv, zsum, zsum_recv, scal, scal_recv,
+    sums, half_sum, half_recv, scal, scal_recv,
     ring_send, ring_recv, sib_send, sib_recv, xo_send, xo_recv, rs_ssem, rs_rsem, ag_ssem, ag_rsem,
-    s_ssem, s_rsem, p_ssem, p_rsem, in_sem,
+    near_rsem, fwd_ssem, s_ssem, s_rsem, p_ssem, p_rsem, in_sem,
 ):
     rows, cols = o_ref.shape
     dom, sub = lax.axis_index("dom"), lax.axis_index("sub")
@@ -113,8 +113,7 @@
     def sub_index(dx, dy):
         return (pair + dx) % 2 * 4 + (y + dy) % 4
 
-    zs = [at(0, dz, 0) for dz in range(1, 8)]
-    right, left, sibling, other = zs[0], zs[6], at(0, 0, 1), at(1, 0, 0)
+    right, left, sibling, other = at(0, 1, 0), at(0, 7, 0), at(0, 0, 1), at(1, 0, 0)
     sub_at = [sub_index(dx, dy) for dx, dy in SUBS]
     subs = [(dom, i) for i in sub_at]
 
@@ -125,7 +124,7 @@
     for move in moves:
         move.start()
     barrier = pltpu.get_barrier_semaphore()
-    partners = zs + [sibling, other] + subs
+    partners = [right, left, sibling, other] + subs
     for partner in partners:
         pl.semaphore_signal(barrier, inc=1, device_id=partner, device_id_type=MESH)
     for move in moves:
@@ -169,11 +168,27 @@
 
         def gram(g):
             a = jnp.concatenate([hx[s, e, d] for d, e in members(g)], axis=0)
-            norms = jnp.sum(a * a, axis=1, keepdims=True)
+            squares = a * a
+            for k, b in enumerate((a, squares)):
+                folded = jnp.sum(b.reshape(b.shape[0] // 8, 8, cols), axis=0)
+                sums[k] = folded if g == 0 else sums[k] + folded
+            norms = jnp.sum(squares, axis=1, keepdims=True)
             norms = jnp.broadcast_to(norms, (a.shape[0], 128)).T[0:1]
             part[s, g] = dot3((jh[...], jl[...]), split(a), NT) + norms_j + norms
             for i in range(7):
                 rs_copy(g, i).start()
+
+        def near_copy(g):
+            here = dist.at[s, g, mine]
+            return copy_to(here, here, ag_ssem.at[s, g], near_rsem.at[s, g], subs[3])
+
+        def forward(g):
+            @pl.when(adds_other == 1)
+            def _():
+                here = dist.at[s, g, pl.ds(pl.multiple_of(((pair + 1) % 2 * 4 + y) * piece, 8), piece)]
+                wait_bytes(here, near_rsem.at[s, g])
+                for i in range(3):
+                    copy_to(here, here, fwd_ssem.at[s, g], ag_rsem.at[s, g, 1], subs[i]).start()
 
         def add_up(g):
             wait_bytes(rs_recv.at[s, g], rs_rsem.at[s, g])
@@ -181,8 +196,17 @@
             for i in range(7):
                 total = total + rs_recv[s, g, i]
             dist[s, g, mine] = total
-            for i in range(7):
+            for i in range(3):
                 ag_copy(g, i).start()
+
+            @pl.when(adds_other == 1)
+            def _():
+                for i in range(3, 7):
+                    ag_copy(g, i).start()
+
+            @pl.when(adds_other == 0)
+            def _():
+                near_copy(g).start()
 
         def add_up_if(kind, *groups):
             @pl.when(adds_other == kind)
@@ -191,6 +215,10 @@
                     add_up(g)
 
         def wait_rows(g, kind):
+            if kind == 0:
+                wait_bytes(dist.at[s, g, pl.ds(0, 3 * piece)], ag_rsem.at[s, g, adds_other])
+                return
+
             @pl.when(adds_other == kind)
             def _():
                 wait_bytes(dist.at[s, g, pl.ds(0, 3 * piece)], ag_rsem.at[s, g, 0])
@@ -199,14 +227,11 @@
             def _():
                 wait_bytes(dist.at[s, g, pl.ds(0, 4 * piece)], ag_rsem.at[s, g, 1])
 
-        def jsum_copy():
-            return copy_to(jsum.at[s], jsum_recv.at[s], s_ssem.at[s, 0], s_rsem.at[s, 0], sibling)
-
-        def zsum_copy(i):
-            return copy_to(zsum.at[s], zsum_recv.at[s, i], s_ssem.at[s, 1], s_rsem.at[s, 1], zs[i])
+        def half_copy():
+            return copy_to(half_sum.at[s], half_recv.at[s], s_ssem.at[s, 0], s_rsem.at[s, 0], other)
 
         def scal_copy(i):
-            return copy_to(scal.at[s], scal_recv.at[s, i], s_ssem.at[s, 2], s_rsem.at[s, 2], subs[i])
+            return copy_to(scal.at[s], scal_recv.at[s, i], s_ssem.at[s, 1], s_rsem.at[s, 1], subs[i])
 
         ring.advance(1)
         ring.hand(1, 7)
@@ -217,19 +242,11 @@
         jx[other_rows] = xo[s]
         js = jx[...]
         jh[...], jl[...] = split(-2.0 * js)
-        squares = js * js
-        norms_j = jnp.sum(squares, axis=1, keepdims=True)
-        sums = [jnp.sum(a, axis=0, keepdims=True) for a in (js, squares)]
-        jsum[s] = jnp.concatenate([a[:, k * 128 : k * 128 + 128] for a in sums for k in range(4)], axis=0)
-        jsum_copy().start()
+        norms_j = jnp.sum(js * js, axis=1, keepdims=True)
 
         ring.advance(2, (0, 1))
         ring.wait_handed(1, 7)
         gram(0)
-        jsum_copy().wait_recv()
-        zsum[s] = jsum[s] + jsum_recv[s]
-        for i in range(7):
-            zsum_copy(i).start()
         ring.advance(2, (2, 3))
         ring.hand(2, 6)
         ring.advance(3, (0,))
@@ -247,26 +264,27 @@
         ring.advance(4)
         ring.hand(4)
         add_up_if(1, 1)
-        wait_bytes(zsum_recv.at[s], s_rsem.at[s, 1])
-        both = zsum[s]
-        for i in range(7):
-            both = both + zsum_recv[s, i]
+        ring.wait_handed(0, 4)
+        gram(3)
+        whole_sums = [jnp.sum(sums[k], axis=0, keepdims=True) for k in range(2)]
+        half_sum[s] = jnp.concatenate([a[:, k * 128 : k * 128 + 128] for a in whole_sums for k in range(4)], axis=0)
+        half_copy().start()
+        if s == 0:
+            ring_g.advance(1)
+            ring_g.hand(1, 7)
+        add_up_if(1, 2)
+        half_copy().wait_recv()
+        both = half_sum[s] + half_recv[s]
         scal[s, 0:4] = both[0:4] * both[0:4]
         scal[s, 4:8] = both[4:8]
         for i in range(7):
             scal_copy(i).start()
-        ring.wait_handed(0, 4)
-        gram(3)
-        if s == 0:
-            ring_g.advance(1)
-            ring_g.hand(1, 7)
-        add_up_if(1, 2)
         if s == 0:
             ring_g.advance(2)
             ring_g.hand(2, 6)
         add_up_if(1, 3)
         add_up_if(0, 0, 1, 2, 3)
-        wait_bytes(scal_recv.at[s], s_rsem.at[s, 2])
+        wait_bytes(scal_recv.at[s], s_rsem.at[s, 1])
         both = scal[s]
         for i in range(7):
             both = both + scal_recv[s, i]
@@ -315,10 +333,13 @@
             if s == 0 and g == 0:
                 ring_g.advance(3)
                 ring_g.hand(3, 5)
+            if g == 3:
+                forward(3)
             targets(g)
             k = weights(g, 1)
             if g < 3:
                 pulled(g, 1, k, whole)
+                forward(g)
             if s == 0 and g == 1:
                 ring_g.advance(4)
                 ring_g.hand(4)
@@ -352,10 +373,17 @@
             t_copy().wait_send()
             for g in range(4):
                 wait_bytes(part.at[s, g, pl.ds(0, 7 * piece)], rs_ssem.at[s, g])
-                wait_bytes(part.at[s, g, pl.ds(0, 7 * piece)], ag_ssem.at[s, g])
-            jsum_copy().wait_send()
-            wait_bytes(zsum_recv.at[s], s_ssem.at[s, 1])
-            wait_bytes(scal_recv.at[s], s_ssem.at[s, 2])
+
+                @pl.when(adds_other == 1)
+                def _():
+                    wait_bytes(part.at[s, g, pl.ds(0, 7 * piece)], ag_ssem.at[s, g])
+                    wait_bytes(part.at[s, g, pl.ds(0, 3 * piece)], fwd_ssem.at[s, g])
+
+                @pl.when(adds_other == 0)
+                def _():
+                    wait_bytes(part.at[s, g, pl.ds(0, 4 * piece)], ag_ssem.at[s, g])
+            half_copy().wait_send()
+            wait_bytes(scal_recv.at[s], s_ssem.at[s, 1])
 
         return drain
 
@@ -397,10 +425,9 @@
             pltpu.VMEM((2, 128, 128), F32),
             pltpu.VMEM((2, 8, 128), F32),
             pltpu.VMEM((2, 8, 128), F32),
+            pltpu.VMEM((2, 8, cols), F32),
             pltpu.VMEM((2, 8, 128), F32),
             pltpu.VMEM((2, 8, 128), F32),
-            pltpu.VMEM((2, 8, 128), F32),
-            pltpu.VMEM((2, 7, 8, 128), F32),
             pltpu.VMEM((2, 8, 128), F32),
             pltpu.VMEM((2, 7, 8, 128), F32),
             dma((3, 2, 4)),
@@ -413,8 +440,10 @@
             dma((2, 4)),
             dma((2, 4)),
             dma((2, 4, 2)),
-            dma((2, 3)),
-            dma((2, 3)),
+            dma((2, 4)),
+            dma((2, 4)),
+            dma((2, 2)),
+            dma((2, 2)),
             dma((2, 3)),
             dma((2, 3)),
             dma((3,)),

time: 101 us -> 99.5 us (0.985)
  Pallas kernels: 99.1 us -> 97.6 us
    pallas_call x1, Pallas kernels: 99.1 us -> 97.6 us  [shards(): pl.pallas_call(kernel, name='stein', out_shape=jax.ShapeDtypeStruct((rows...]
where the time goes in v3:
time: 99.5 us; the launch traced here: 99.2 us
  Pallas kernels  97.6 us (98%)
  local copies, waits for them, and re-layouts  1.62 us (2%)
    pallas_call x1, Pallas kernels, shards(): pl.pallas_call(kernel, name='stein', out_shape=jax.ShapeDtypeStruct((rows...  97.6 us

profile of v3, /device:TPU:1, one launch (start us, length us, event | category | flops | bytes accessed | tf_op | source)
XLA Modules:
  0.0 99.2 jit_solution(14937636859974169764)
XLA Ops:
  0.0 97.6 %stein.1 = f32[96,512]{1,0:T(8,128)} custom-call(f32[96,512]{1,0:T(8,128)} %x_ref.1, f32[96,512]{1,0:T(8,128)} %g_ref.1, f32[1,512]{1,0:T(1,128)} %bitcast.1), custom_call_target="tpu_custom_call" | custom-call | tf_op jit(solution)/shard_map/stein/pallas_call | solution.py:404
  97.6 1.6 %copy.5 = f32[96,512]{1,0:T(8,128)} copy(f32[96,512]{1,0:T(8,128)} %stein.1) | data formatting | bytes 393216

commit v4 on v3

--- a/solution.py
+++ b/solution.py
@@ -74,6 +74,16 @@
     def hand(self, *blocks):
         for d in blocks:
             self.sib_copy(d).start()
+
+    def finish(self):
+        width = self.held.shape[3] // 2
+        for hf in range(2):
+            self.advance(4, (2 * hf, 2 * hf + 1))
+            lanes = pl.ds(hf * width, width)
+            copy_to(
+                self.held.at[0, 4, :, lanes], self.held.at[1, 4, :, lanes], self.sib_send.at[4], self.sib_recv.at[4],
+                self.sibling,
+            ).start()
 
     def wait_handed(self, *blocks):
         for d in blocks:
@@ -175,8 +185,16 @@
             norms = jnp.sum(squares, axis=1, keepdims=True)
             norms = jnp.broadcast_to(norms, (a.shape[0], 128)).T[0:1]
             part[s, g] = dot3((jh[...], jl[...]), split(a), NT) + norms_j + norms
-            for i in range(7):
-                rs_copy(g, i).start()
+
+            @pl.when(adds_other == 1)
+            def _():
+                for i in range(7):
+                    rs_copy(g, i).start()
+
+            @pl.when(adds_other == 0)
+            def _():
+                for i in (3, 4, 5, 6, 0, 1, 2):
+                    rs_copy(g, i).start()
 
         def near_copy(g):
             here = dist.at[s, g, mine]
@@ -261,8 +279,7 @@
             ring_g.hand(0)
         ring.wait_handed(3, 5)
         gram(2)
-        ring.advance(4)
-        ring.hand(4)
+        ring.finish()
         add_up_if(1, 1)
         ring.wait_handed(0, 4)
         gram(3)

time: 99.5 us -> 99.5 us (level)
  no operation moved by 1% of the time
where the time goes in v4:
time: 99.5 us; the launch traced here: 99 us
  Pallas kernels  97.4 us (98%)
  local copies, waits for them, and re-layouts  1.62 us (2%)
    pallas_call x1, Pallas kernels, shards(): pl.pallas_call(kernel, name='stein', out_shape=jax.ShapeDtypeStruct((rows...  97.4 us

profile of v4, /device:TPU:1, one launch (start us, length us, event | category | flops | bytes accessed | tf_op | source)
XLA Modules:
  0.0 99.0 jit_solution(4904395072999087279)
XLA Ops:
  0.0 97.4 %stein.1 = f32[96,512]{1,0:T(8,128)} custom-call(f32[96,512]{1,0:T(8,128)} %x_ref.1, f32[96,512]{1,0:T(8,128)} %g_ref.1, f32[1,512]{1,0:T(1,128)} %bitcast.1), custom_call_target="tpu_custom_call" | custom-call | tf_op jit(solution)/shard_map/stein/pallas_call | solution.py:421
  97.4 1.6 %copy.5 = f32[96,512]{1,0:T(8,128)} copy(f32[96,512]{1,0:T(8,128)} %stein.1) | data formatting | bytes 393216
